TPU v7x, 256 devices: a whole 4x4x8 slice. The times are simulated.
256 devices in a mesh: outer: 32 (over z, x_lo, core), inner: 8 (over x_hi, y).
Axes of the slice: x: 4 (x_hi: 2, x_lo: 2; x = x_hi * 2 + x_lo), y: 4, z: 8, core: 2. Of those that a mesh axis runs over, the one named last changes fastest.
Arguments:
- queries: bfloat16 [65536, 4096], P(('outer', 'inner')), may hold values from -136 to 136
- keys: bfloat16 [65536, 512], P(('outer', 'inner')), may hold values from -6 to 6
- values: bfloat16 [65536, 512], P(('outer', 'inner')), may hold values from -6 to 6
- segment: int32 [65536], P(('outer', 'inner')), may hold values from 0 to 31, never falling along the last dimension, each value on 1 to 4096 neighbouring positions
- signs: int32 [128], replicated, may hold values from 0 to 1
Outputs:
- attended: bfloat16 [65536, 4096], P(('outer', 'inner'))
Inputs may be any that keep to these rules, and one draw needn't show every extreme that they name: `segment`: document numbers never fall along the sequence; each document holds 1 to 4096 tokens, and one holds exactly that many.
All inputs are finite; a program needn't handle non-finite values.
Results may differ from a plain program's by a relative error of at most 0.0057.
Values may be sent and summed in bfloat16 or wider, within the bound.
A program may use at most 192 MiB of HBM per device.

v0:
```python
import jax
import jax.numpy as jnp
import numpy as np
from jax import lax
from jax.sharding import PartitionSpec as P


def shifted(array, axis, by):
    count = lax.axis_size(axis)
    pairs = [(i, i + by) for i in range(count) if 0 <= i + by < count]
    return lax.ppermute(array, axis, pairs)


def hadamard_table(order):
    table = np.ones((1, 1))
    while table.shape[0] < order:
        upper = np.concatenate([table, table], axis=1)
        lower = np.concatenate([table, -table], axis=1)
        table = np.concatenate([upper, lower], axis=0)
    return table / np.sqrt(order)


def rotate(values, signs):
    head_size = signs.shape[0]
    heads = values.shape[1] // head_size
    flips = (1 - 2 * signs).astype(jnp.float32)
    scaled = values.astype(jnp.float32).reshape(-1, heads, head_size) * flips
    table = jnp.asarray(hadamard_table(head_size), jnp.float32)
    turned = jnp.dot(scaled.reshape(-1, head_size), table, precision=lax.Precision.HIGHEST)
    return turned.reshape(values.shape[0], heads * head_size).astype(jnp.bfloat16)


def tile_scores(query_grouped, key_row_block, head_size):
    sequence_length = key_row_block.shape[0]
    heads_kv = query_grouped.shape[1]
    key_grouped = key_row_block.reshape(sequence_length, heads_kv, head_size)
    scores = jnp.einsum(
        "bhgd,lhd->hgbl", query_grouped, key_grouped, preferred_element_type=jnp.float32
    )
    return scores / jnp.sqrt(jnp.float32(head_size))


def on_device(queries, keys, values, segment, signs):
    head_size = signs.shape[0]
    token_rows = queries.shape[0]
    heads_kv = keys.shape[1] // head_size
    heads_q = queries.shape[1] // head_size
    query_group = heads_q // heads_kv
    n_inner = lax.axis_size("inner")
    block = lax.axis_index("outer") * n_inner + lax.axis_index("inner")
    rotated = rotate(values, signs)
    seg_wire = segment.astype(jnp.bfloat16)
    packet = (keys, rotated, seg_wire)
    near = shifted((keys, rotated, seg_wire), ("outer", "inner"), 1)
    hop = shifted((keys, rotated, seg_wire), "outer", 1)
    far = shifted((keys, rotated, seg_wire), ("outer", "inner"), n_inner + 1)
    query_grouped = queries.reshape(token_rows, heads_kv, query_group, head_size)
    row_index = jnp.arange(token_rows, dtype=jnp.int32)
    pieces = [(packet, 0), (near, 1), (hop, n_inner), (far, n_inner + 1)]
    score_list, mask_list, value_list = ([], [], [])
    for piece, offset in pieces:
        score_list.append(tile_scores(query_grouped, piece[0], head_size))
        allowed = (seg_wire[:, None] == piece[2][None, :]) & (block - offset >= 0)
        if offset == 0:
            allowed = allowed & (row_index[:, None] >= row_index[None, :])
        mask_list.append(allowed)
        value_list.append(piece[1])
    scores = jnp.concatenate(score_list, axis=-1)
    visible = jnp.concatenate(mask_list, axis=1)
    scores = jnp.where(visible[None, None], scores, jnp.float32(-1e30))
    top = jnp.max(scores, axis=-1, keepdims=True)
    expo = jnp.exp(scores - top)
    total = jnp.sum(expo, axis=-1, keepdims=True)
    weights = (expo / total).astype(jnp.bfloat16)
    value_row_block = jnp.concatenate(value_list, axis=0).reshape(-1, heads_kv, head_size)
    mixed = jnp.einsum(
        "hgbl,lhd->bhgd", weights, value_row_block, preferred_element_type=jnp.float32
    )
    return mixed.reshape(token_rows, heads_q * head_size).astype(jnp.bfloat16)


def solution(mesh):
    placed = (
        P(("outer", "inner"), None),
        P(("outer", "inner"), None),
        P(("outer", "inner"), None),
        P(("outer", "inner")),
        P(),
    )
    return jax.shard_map(
        on_device,
        mesh=mesh,
        in_specs=placed,
        out_specs=P(("outer", "inner"), None),
        check_vma=False,
    )
```

profile of v0, /device:TPU:75, one launch (start us, length us, event | category | flops | bytes accessed | tf_op | source)
XLA Modules:
  0.0 99.7 jit_solution(4215429205724296646)
XLA Ops:
  0.0 0.7 convert_element_type.28
  0.7 3.2 %collective-permute-start.3 = (bf16[256]{0:T(256)(128)(2,1)S(1)}, bf16[256]{0:T(256)(128)(2,1)S(1)}, u32[]{:S(2)}, u32[]{:S(2)}) collective-permute-start(bf16[256]{0:T(256)(128)(2,1)S(1)} %convert_element_type.28), channel_id=1, source_target_pairs={{0,1},{1,2},{2,3},{3,4},{4,5},{5,6},{6,7},{7,8},{8,9},{9,10},{10,1... | collective-permute-start | bytes 1544 | tf_op jit(solution)/shard_map/ppermute | solution.py:11
  3.9 4.4 %collective-permute-start.4 = (bf16[256]{0:T(256)(128)(2,1)S(1)}, bf16[256]{0:T(256)(128)(2,1)S(1)}, u32[]{:S(2)}, u32[]{:S(2)}) collective-permute-start(bf16[256]{0:T(256)(128)(2,1)S(1)} %convert_element_type.28), channel_id=1, source_target_pairs={{0,8},{8,16},{16,24},{24,32},{32,40},{40,48},{48,56},{56,64},{64,7... | collective-permute-start | bytes 1544 | tf_op jit(solution)/shard_map/ppermute | solution.py:11
  8.2 2.6 %collective-permute-start.5 = (bf16[256]{0:T(256)(128)(2,1)S(1)}, bf16[256]{0:T(256)(128)(2,1)S(1)}, u32[]{:S(2)}, u32[]{:S(2)}) collective-permute-start(bf16[256]{0:T(256)(128)(2,1)S(1)} %convert_element_type.28), channel_id=1, source_target_pairs={{0,9},{1,10},{2,11},{3,12},{4,13},{5,14},{6,15},{7,16},{8,17},{9,1... | collective-permute-start | bytes 1544 | tf_op jit(solution)/shard_map/ppermute | solution.py:11
  10.9 1.8 %copy.18 = bf16[256,512]{0,1:T(8,128)(2,1)} copy(bf16[256,512]{1,0:T(8,128)(2,1)} %param.7) | data formatting | bytes 524288 | tf_op args[1]
  12.7 4.9 %collective-permute-start.8 = (bf16[256,512]{0,1:T(8,128)(2,1)}, bf16[256,512]{0,1:T(8,128)(2,1)S(1)}, u32[]{:S(2)}, u32[]{:S(2)}) collective-permute-start(bf16[256,512]{0,1:T(8,128)(2,1)} %copy.18), channel_id=1, source_target_pairs={{0,9},{1,10},{2,11},{3,12},{4,13},{5,14},{6,15},{7,16},{8,17},{9,1... | collective-permute-start | bytes 786440 | tf_op jit(solution)/shard_map/ppermute | solution.py:11
  17.6 1.9 %collective-permute-start.7 = (bf16[256,512]{0,1:T(8,128)(2,1)}, bf16[256,512]{0,1:T(8,128)(2,1)S(1)}, u32[]{:S(2)}, u32[]{:S(2)}) collective-permute-start(bf16[256,512]{0,1:T(8,128)(2,1)} %copy.18), channel_id=1, source_target_pairs={{0,8},{8,16},{16,24},{24,32},{32,40},{40,48},{48,56},{56,64},{64,7... | collective-permute-start | bytes 786440 | tf_op jit(solution)/shard_map/ppermute | solution.py:11
  19.5 1.0 %reshape.42 = bf16[256,4,128]{2,1,0:T(4,128)(2,1)S(1)} reshape(bf16[256,512]{1,0:T(8,128)(2,1)} %param.7) | data formatting | bytes 524288 | tf_op jit(solution)/shard_map/reshape | solution.py:36
  20.5 2.1 %copy.43 = bf16[32,8,32,128]{3,2,1,0:T(8,128)(2,1)S(1)} copy(bf16[32,8,32,128]{3,1,2,0:T(8,128)(2,1)} %bitcast.44) | data formatting | bytes 4194304
  22.6 0.0 copy-start.1
  22.6 1.1 %reshape.48 = f32[1024,128]{1,0:T(8,128)S(1)} reshape(bf16[256,512]{1,0:T(8,128)(2,1)} %param.8) | data formatting | bytes 786432 | tf_op jit(solution)/shard_map/reshape | solution.py:27
  23.8 0.7 subtract_convert_fusion
  24.4 4.9 %multiply_bitcast_fusion.3 = f32[4,8,256,256]{2,3,1,0:T(8,128)} fusion(bf16[256,4,8,128]{3,2,1,0:T(8,128)(2,1)S(1)} %bitcast.40, bf16[256,4,128,1]{2,1,0,3:T(4,128)(2,1)S(1)} %bitcast.46), kind=kOutput, calls=%fused_computation.11 | convolution fusion | flops 538968064 | bytes 10747904 | tf_op jit(solution)/shard_map/bhgd,lhd->hgbl/dot_general | solution.py:37
  29.3 0.6 convolution_convert_fusion
  29.9 0.2 convert_element_type.27
  30.0 0.0 collective-permute-done.3
  30.0 3.8 %collective-permute-start.6 = (bf16[256,512]{0,1:T(8,128)(2,1)}, bf16[256,512]{0,1:T(8,128)(2,1)S(1)}, u32[]{:S(2)}, u32[]{:S(2)}) collective-permute-start(bf16[256,512]{0,1:T(8,128)(2,1)} %copy.18), channel_id=1, source_target_pairs={{0,1},{1,2},{2,3},{3,4},{4,5},{5,6},{6,7},{7,8},{8,9},{9,10},{10,1... | collective-permute-start | bytes 786440 | tf_op jit(solution)/shard_map/ppermute | solution.py:11
  33.9 0.0 collective-permute-done.4
  33.9 3.2 %collective-permute-start = (bf16[256,512]{1,0:T(8,128)(2,1)S(1)}, bf16[256,512]{1,0:T(8,128)(2,1)S(1)}, u32[]{:S(2)}, u32[]{:S(2)}) collective-permute-start(bf16[256,512]{1,0:T(8,128)(2,1)S(1)} %convert_element_type.27), channel_id=1, source_target_pairs={{0,1},{1,2},{2,3},{3,4},{4,5},{5,6},{6,7},{7,8},{8,9},{9,10},{10,1... | collective-permute-start | bytes 786440 | tf_op jit(solution)/shard_map/ppermute | solution.py:11
  37.1 0.0 collective-permute-done.5
  37.1 5.1 %collective-permute-start.1 = (bf16[256,512]{1,0:T(8,128)(2,1)S(1)}, bf16[256,512]{1,0:T(8,128)(2,1)S(1)}, u32[]{:S(2)}, u32[]{:S(2)}) collective-permute-start(bf16[256,512]{1,0:T(8,128)(2,1)S(1)} %convert_element_type.27), channel_id=1, source_target_pairs={{0,8},{8,16},{16,24},{24,32},{32,40},{40,48},{48,56},{56,64},{64,7... | collective-permute-start | bytes 786440 | tf_op jit(solution)/shard_map/ppermute | solution.py:11
  42.2 0.3 fusion.13
  42.4 0.7 pad_add_fusion
  43.2 3.7 %collective-permute-start.2 = (bf16[256,512]{1,0:T(8,128)(2,1)S(1)}, bf16[256,512]{1,0:T(8,128)(2,1)S(1)}, u32[]{:S(2)}, u32[]{:S(2)}) collective-permute-start(bf16[256,512]{1,0:T(8,128)(2,1)S(1)} %convert_element_type.27), channel_id=1, source_target_pairs={{0,9},{1,10},{2,11},{3,12},{4,13},{5,14},{6,15},{7,16},{8,17},{9,1... | collective-permute-start | bytes 786440 | tf_op jit(solution)/shard_map/ppermute | solution.py:11
  46.9 4.7 %multiply_bitcast_fusion = f32[4,8,256,256]{2,3,1,0:T(8,128)} fusion(bf16[256,4,128,1]{0,2,3,1:T(8,128)(2,1)S(1)} %bitcast.49, bf16[256,4,8,128]{3,2,1,0:T(8,128)(2,1)S(1)} %bitcast.41), kind=kOutput, calls=%fused_computation.8 | convolution fusion | flops 538968064 | bytes 10747904 | tf_op jit(solution)/shard_map/bhgd,lhd->hgbl/dot_general | solution.py:37
  51.6 4.7 %multiply_bitcast_fusion.1 = f32[4,8,256,256]{2,3,1,0:T(8,128)} fusion(bf16[256,4,128,1]{0,2,3,1:T(8,128)(2,1)S(1)} %bitcast.48, bf16[256,4,8,128]{3,2,1,0:T(8,128)(2,1)S(1)} %bitcast.42), kind=kOutput, calls=%fused_computation.9 | convolution fusion | flops 538968064 | bytes 10747904 | tf_op jit(solution)/shard_map/bhgd,lhd->hgbl/dot_general | solution.py:37
  56.3 4.7 %multiply_bitcast_fusion.2 = f32[4,8,256,256]{2,3,1,0:T(8,128)} fusion(bf16[256,4,128,1]{0,2,3,1:T(8,128)(2,1)S(1)} %bitcast.50, bf16[256,4,8,128]{3,2,1,0:T(8,128)(2,1)S(1)} %bitcast.43), kind=kOutput, calls=%fused_computation.10 | convolution fusion | flops 538968064 | bytes 10747904 | tf_op jit(solution)/shard_map/bhgd,lhd->hgbl/dot_general | solution.py:37
  61.0 0.1 pad_maximum_fusion
  61.1 0.5 copy.15
  61.7 23.3 %fusion.16 = (f32[4,8,256]{2,1,0:T(8,128)S(1)}, f32[4,8,256,1024]{2,3,1,0:T(8,128)}) fusion(f32[4,8,256,256]{2,3,1,0:T(8,128)} %multiply_bitcast_fusion, f32[4,8,256,256]{2,3,1,0:T(8,128)} %multiply_bitcast_fusion.1, f32[4,8,256,256]{2,3,1,0:T(8,128)} %multiply_bitcast_fusion.2, f32[4,8,256,256]{2,3,1,0:T(8,128)} %multiply_bitcast_fusion.3, ...), kind=kOutput, calls=%fused_computation.31 | output fusion | flops 50332672 | bytes 67403776 | tf_op jit(solution)/shard_map/sub | solution.py:72
  84.9 11.9 %fusion.5 = bf16[4,128,8,256]{3,1,2,0:T(8,128)(2,1)S(1)} fusion(bf16[1024,4,128,1]{0,2,3,1:T(8,128)(2,1)S(1)} %bitcast.47, f32[4,8,256,1024]{2,3,1,0:T(8,128)} %get-tuple-element.10, f32[4,8,256]{2,1,0:T(8,128)S(1)} %get-tuple-element.9), kind=kOutput, calls=%fused_computation.12 | convolution fusion | flops 2165309440 | bytes 36732928 | tf_op jit(solution)/shard_map/hgbl,lhd->bhgd/dot_general | solution.py:76
  96.8 2.9 %copy.28 = bf16[256,4096]{1,0:T(8,128)(2,1)} copy(bf16[256,4096]{0,1:T(8,128)(2,1)S(1)} %bitcast.45) | data formatting | bytes 4194304 | tf_op jit(solution)/shard_map/convert_element_type | solution.py:79
  (9 shorter events, 0.0 us)
Async XLA Ops:
  0.7 29.4 %collective-permute-start.3 = (bf16[256]{0:T(256)(128)(2,1)S(1)}, bf16[256]{0:T(256)(128)(2,1)S(1)}, u32[]{:S(2)}, u32[]{:S(2)}) collective-permute-start(bf16[256]{0:T(256)(128)(2,1)S(1)} %convert_element_type.28), channel_id=1, source_target_pairs={{0,1},{1,2},{2,3},{3,4},{4,5},{5,6},{6,7},{7,8},{8,9},{9,10},{10,1... | collective-permute-start | bytes 1544 | tf_op jit(solution)/shard_map/ppermute | solution.py:11
  3.9 30.0 %collective-permute-start.4 = (bf16[256]{0:T(256)(128)(2,1)S(1)}, bf16[256]{0:T(256)(128)(2,1)S(1)}, u32[]{:S(2)}, u32[]{:S(2)}) collective-permute-start(bf16[256]{0:T(256)(128)(2,1)S(1)} %convert_element_type.28), channel_id=1, source_target_pairs={{0,8},{8,16},{16,24},{24,32},{32,40},{40,48},{48,56},{56,64},{64,7... | collective-permute-start | bytes 1544 | tf_op jit(solution)/shard_map/ppermute | solution.py:11
  8.2 28.8 %collective-permute-start.5 = (bf16[256]{0:T(256)(128)(2,1)S(1)}, bf16[256]{0:T(256)(128)(2,1)S(1)}, u32[]{:S(2)}, u32[]{:S(2)}) collective-permute-start(bf16[256]{0:T(256)(128)(2,1)S(1)} %convert_element_type.28), channel_id=1, source_target_pairs={{0,9},{1,10},{2,11},{3,12},{4,13},{5,14},{6,15},{7,16},{8,17},{9,1... | collective-permute-start | bytes 1544 | tf_op jit(solution)/shard_map/ppermute | solution.py:11
  12.7 30.5 %collective-permute-start.8 = (bf16[256,512]{0,1:T(8,128)(2,1)}, bf16[256,512]{0,1:T(8,128)(2,1)S(1)}, u32[]{:S(2)}, u32[]{:S(2)}) collective-permute-start(bf16[256,512]{0,1:T(8,128)(2,1)} %copy.18), channel_id=1, source_target_pairs={{0,9},{1,10},{2,11},{3,12},{4,13},{5,14},{6,15},{7,16},{8,17},{9,1... | collective-permute-start | bytes 786440 | tf_op jit(solution)/shard_map/ppermute | solution.py:11
  17.6 34.0 %collective-permute-start.7 = (bf16[256,512]{0,1:T(8,128)(2,1)}, bf16[256,512]{0,1:T(8,128)(2,1)S(1)}, u32[]{:S(2)}, u32[]{:S(2)}) collective-permute-start(bf16[256,512]{0,1:T(8,128)(2,1)} %copy.18), channel_id=1, source_target_pairs={{0,8},{8,16},{16,24},{24,32},{32,40},{40,48},{48,56},{56,64},{64,7... | collective-permute-start | bytes 786440 | tf_op jit(solution)/shard_map/ppermute | solution.py:11
  22.6 6.7 %copy-start.1 = (f32[128,128]{1,0:T(8,128)S(1)}, f32[128,128]{1,0:T(8,128)}, u32[]{:S(2)}) copy-start(f32[128,128]{1,0:T(8,128)} %constant.39.clone) | copy-start | bytes 196612
  30.0 26.3 %collective-permute-start.6 = (bf16[256,512]{0,1:T(8,128)(2,1)}, bf16[256,512]{0,1:T(8,128)(2,1)S(1)}, u32[]{:S(2)}, u32[]{:S(2)}) collective-permute-start(bf16[256,512]{0,1:T(8,128)(2,1)} %copy.18), channel_id=1, source_target_pairs={{0,1},{1,2},{2,3},{3,4},{4,5},{5,6},{6,7},{7,8},{8,9},{9,10},{10,1... | collective-permute-start | bytes 786440 | tf_op jit(solution)/shard_map/ppermute | solution.py:11
  33.9 27.2 %collective-permute-start = (bf16[256,512]{1,0:T(8,128)(2,1)S(1)}, bf16[256,512]{1,0:T(8,128)(2,1)S(1)}, u32[]{:S(2)}, u32[]{:S(2)}) collective-permute-start(bf16[256,512]{1,0:T(8,128)(2,1)S(1)} %convert_element_type.27), channel_id=1, source_target_pairs={{0,1},{1,2},{2,3},{3,4},{4,5},{5,6},{6,7},{7,8},{8,9},{9,10},{10,1... | collective-permute-start | bytes 786440 | tf_op jit(solution)/shard_map/ppermute | solution.py:11
  37.1 23.9 %collective-permute-start.1 = (bf16[256,512]{1,0:T(8,128)(2,1)S(1)}, bf16[256,512]{1,0:T(8,128)(2,1)S(1)}, u32[]{:S(2)}, u32[]{:S(2)}) collective-permute-start(bf16[256,512]{1,0:T(8,128)(2,1)S(1)} %convert_element_type.27), channel_id=1, source_target_pairs={{0,8},{8,16},{16,24},{24,32},{32,40},{40,48},{48,56},{56,64},{64,7... | collective-permute-start | bytes 786440 | tf_op jit(solution)/shard_map/ppermute | solution.py:11
  43.2 17.9 %collective-permute-start.2 = (bf16[256,512]{1,0:T(8,128)(2,1)S(1)}, bf16[256,512]{1,0:T(8,128)(2,1)S(1)}, u32[]{:S(2)}, u32[]{:S(2)}) collective-permute-start(bf16[256,512]{1,0:T(8,128)(2,1)S(1)} %convert_element_type.27), channel_id=1, source_target_pairs={{0,9},{1,10},{2,11},{3,12},{4,13},{5,14},{6,15},{7,16},{8,17},{9,1... | collective-permute-start | bytes 786440 | tf_op jit(solution)/shard_map/ppermute | solution.py:11
  56.3 5.4 %copy-start = (pred[256,1024]{0,1:T(8,128)(4,1)S(1)}, pred[256,1024]{0,1:T(8,128)(4,1)}, u32[]{:S(2)}) copy-start(pred[256,1024]{0,1:T(8,128)(4,1)} %pad_add_fusion) | copy-start | bytes 786436
where the time goes:
time: 100 us; the launch traced here: 99.7 us
  starting transfers between devices  32.8 us (33%)
  matrix products  31.4 us (31%)
  other arithmetic  25.6 us (26%)
  local copies, waits for them, and re-layouts  9.58 us (10%)
    ppermute x9, starting transfers between devices, shifted(): return lax.ppermute(array, axis, pairs)  32.8 us
    sub x1, other arithmetic, on_device(): expo = jnp.exp(scores - top)  23.3 us
    dot_general x4, matrix products, tile_scores(): jnp.einsum('bhgd,lhd->hgbl', query_grouped, key_grouped, preferred_elemen...  19 us
    dot_general x1, matrix products, on_device(): jnp.einsum('hgbl,lhd->bhgd', weights, value_row_block, preferred_element_...  11.9 us
    unnamed x6, local copies, waits for them, and re-layouts  3.87 us
    convert_element_type x1, local copies, waits for them, and re-layouts, on_device(): return mixed.reshape(token_rows, heads_q * head_size).astype(jnp.bfloat16)  2.86 us
  transfers between devices with their start and end apart: 9, of which 0 were waited for; matrix products, arithmetic and copies ran while one was open for 27% of the time, Pallas kernels for 0%

commit v1 on v0

v1 whole, which is shorter than its diff:
```python
import functools
import math

import jax
import jax.numpy as jnp
from jax import lax
from jax.experimental import pallas as pl
from jax.experimental.pallas import tpu as pltpu
from jax.sharding import PartitionSpec as P

MESH = pl.DeviceIdType.MESH
BLOCK = 256
HEAD = 128
KV = 4
GROUP = 8
ROWS = 2 * BLOCK + 16
NEG = -1e30
NO_DOC = 127
SCALE = math.log2(math.e) / math.sqrt(HEAD)
ROW_BY_ROW = (((1,), (1,)), ((), ()))
BF16 = jnp.bfloat16
F32 = jnp.float32


def hadamard_signs():
    left = lax.broadcasted_iota(jnp.int32, (HEAD, HEAD), 0)
    right = lax.broadcasted_iota(jnp.int32, (HEAD, HEAD), 1)
    both = left & right
    both = both ^ (both >> 4)
    both = both ^ (both >> 2)
    both = both ^ (both >> 1)
    return (1 - 2 * (both & 1)).astype(F32).astype(BF16)


def documents(packet_rows):
    parts = []
    for half in range(2):
        row = packet_rows[8 * half : 8 * half + 1, :].astype(F32)
        ids = lax.broadcasted_iota(jnp.int32, (HEAD, HEAD), 0).astype(F32)
        parts.append(jnp.where(row == ids, F32(1), F32(0)).T)
    return jnp.concatenate(parts, axis=0)


def kernel(
    n_outer, n_inner, q_hbm, k_hbm, v_hbm, seg_ref, signs_ref, o_hbm,
    q, raw, packs, out, top, acc, bias, away, docs,
    q_sem, k_sem, v_sem, o_sem, send, recv,
):
    me = lax.axis_index("outer") * n_inner + lax.axis_index("inner")
    count = n_outer * n_inner

    def device(index):
        return {"outer": lax.div(index, n_inner), "inner": lax.rem(index, n_inner)}

    offsets = (1, n_inner)
    barrier = pltpu.get_barrier_semaphore()
    for offset in offsets:
        @pl.when(me >= offset)
        def _():
            pl.semaphore_signal(barrier, inc=1, device_id=device(me - offset), device_id_type=MESH)

    def columns(h):
        return pl.ds(h * HEAD, HEAD)

    k_in = [pltpu.make_async_copy(k_hbm.at[:, columns(h)], packs.at[0, h, pl.ds(0, BLOCK)], k_sem.at[h]) for h in range(KV)]
    v_in = [pltpu.make_async_copy(v_hbm.at[:, columns(h)], raw.at[h], v_sem.at[h]) for h in range(KV)]
    wide = GROUP * HEAD
    q_in = [pltpu.make_async_copy(q_hbm.at[:, pl.ds(g * wide, wide)], q.at[g], q_sem.at[g]) for g in range(KV)]
    for copy in v_in + k_in + q_in:
        copy.start()

    seg = seg_ref[...].astype(F32)
    lower = lax.broadcasted_iota(jnp.int32, (16, HEAD), 0) < 8
    own_rows = jnp.where(lower, seg[:, :HEAD], seg[:, HEAD:]).astype(BF16)
    flips = (1 - 2 * signs_ref[...]).astype(F32)
    table = hadamard_signs()

    for h in range(KV):
        v_in[h].wait()
        turned = jnp.dot((raw[h].astype(F32) * flips).astype(BF16), table, preferred_element_type=F32)
        packs[0, h, BLOCK : 2 * BLOCK, :] = (turned * F32(1 / math.sqrt(HEAD))).astype(BF16)
        packs[0, h, 2 * BLOCK :, :] = own_rows
        k_in[h].wait()

    for place, offset in ((1, 1), (2, n_inner), (3, n_inner + 1)):
        @pl.when(me < offset)
        def _():
            for h in range(KV):
                packs[place, h, : 2 * BLOCK, :] = jnp.zeros((2 * BLOCK, HEAD), BF16)
                packs[place, h, 2 * BLOCK :, :] = jnp.full((16, HEAD), NO_DOC, BF16)

    def carry(source, place, h, offset):
        return pltpu.make_async_remote_copy(
            src_ref=packs.at[source, h], dst_ref=packs.at[place, h],
            send_sem=send.at[place - 1, h], recv_sem=recv.at[place - 1, h],
            device_id=device(me + offset), device_id_type=MESH,
        )

    near = [carry(0, 1, h, 1) for h in range(KV)]
    hop = [carry(0, 2, h, n_inner) for h in range(KV)]
    far = [carry(1, 3, h, n_inner) for h in range(KV)]
    has_near, has_hop, has_far = me >= 1, me >= n_inner, me >= n_inner + 1
    to_near, to_hop = me + 1 < count, me + n_inner < count
    to_far = has_near & to_hop

    pl.when(to_hop)(lambda: pl.semaphore_wait(barrier, 2))
    pl.when(to_near & (me + n_inner >= count))(lambda: pl.semaphore_wait(barrier, 1))
    for h in range(KV):
        pl.when(to_near)(near[h].start)
        pl.when(to_hop)(hop[h].start)

    own = documents(packs[0, 0, 2 * BLOCK :, :])
    same = lax.dot_general(own.astype(BF16), own.astype(BF16), ROW_BY_ROW, preferred_element_type=F32)
    row = lax.broadcasted_iota(jnp.int32, (BLOCK, BLOCK), 0)
    column = lax.broadcasted_iota(jnp.int32, (BLOCK, BLOCK), 1)
    bias[...] = jnp.where((same > 0.5) & (row >= column), F32(0), F32(NEG))
    away[...] = jnp.where(own > 0.5, F32(0), F32(NEG)).astype(BF16)
    ones = jnp.ones((BLOCK, HEAD), BF16)

    def values_of(place, g):
        return jnp.concatenate([packs[place, g, BLOCK : 2 * BLOCK, :], ones], axis=1)

    for g in range(KV):
        q_in[g].wait()
        for j in range(GROUP):
            scores = lax.dot_general(
                q[g, :, j * HEAD : (j + 1) * HEAD], packs[0, g, :BLOCK, :], ROW_BY_ROW, preferred_element_type=F32
            ) + bias[...]
            peak = jnp.max(scores, axis=1, keepdims=True)
            weights = jnp.exp2((scores - peak) * SCALE).astype(BF16)
            top[g * GROUP + j] = jnp.broadcast_to(peak, (BLOCK, HEAD))
            acc[g * GROUP + j] = jnp.dot(weights, values_of(0, g), preferred_element_type=F32)

    def arrive(h):
        pl.when(has_near)(near[h].wait_recv)
        pl.when(to_far)(far[h].start)

    def attend(g):
        pl.when(has_hop)(hop[g].wait_recv)
        pl.when(has_far)(far[g].wait_recv)
        if g == 0:
            for place in (1, 2, 3):
                docs[place - 1] = documents(packs[place, 0, 2 * BLOCK :, :]).astype(BF16)
        for j in range(GROUP):
            query = jnp.concatenate([q[g, :, j * HEAD : (j + 1) * HEAD], away[...]], axis=1)
            scores = []
            for place in (1, 2, 3):
                key = jnp.concatenate([packs[place, g, :BLOCK, :], docs[place - 1]], axis=1)
                scores.append(lax.dot_general(query, key, ROW_BY_ROW, preferred_element_type=F32))
            before = top[g * GROUP + j][:, :1]
            peak = jnp.max(functools.reduce(jnp.maximum, scores), axis=1, keepdims=True)
            peak = jnp.maximum(peak, before)
            total = acc[g * GROUP + j] * jnp.exp2((before - peak) * SCALE)
            for place in (1, 2, 3):
                weights = jnp.exp2((scores[place - 1] - peak) * SCALE).astype(BF16)
                total = total + jnp.dot(weights, values_of(place, g), preferred_element_type=F32)
            out[g, :, j * HEAD : (j + 1) * HEAD] = (total[:, :HEAD] / total[:, HEAD:]).astype(BF16)
        copy = pltpu.make_async_copy(out.at[g], o_hbm.at[:, pl.ds(g * wide, wide)], o_sem.at[g])
        copy.start()
        return copy

    arrive(0)
    arrive(1)
    outs = [attend(0)]
    arrive(2)
    outs.append(attend(1))
    arrive(3)
    outs.append(attend(2))
    outs.append(attend(3))
    for h in range(KV):
        pl.when(to_near)(near[h].wait_send)
        pl.when(to_hop)(hop[h].wait_send)
        pl.when(to_far)(far[h].wait_send)
        outs[h].wait()


def solution(mesh):
    n_outer, n_inner = mesh.shape["outer"], mesh.shape["inner"]

    def on_device(queries, keys, values, segment, signs):
        anywhere = pl.BlockSpec(memory_space=pl.ANY)
        here = pl.BlockSpec(memory_space=pltpu.VMEM)
        return pl.pallas_call(
            functools.partial(kernel, n_outer, n_inner),
            out_shape=jax.ShapeDtypeStruct(queries.shape, BF16),
            in_specs=[anywhere, anywhere, anywhere, here, here],
            out_specs=anywhere,
            scratch_shapes=[
                pltpu.VMEM((KV, BLOCK, GROUP * HEAD), BF16),
                pltpu.VMEM((KV, BLOCK, HEAD), BF16),
                pltpu.VMEM((4, KV, ROWS, HEAD), BF16),
                pltpu.VMEM((KV, BLOCK, GROUP * HEAD), BF16),
                pltpu.VMEM((KV * GROUP, BLOCK, HEAD), F32),
                pltpu.VMEM((KV * GROUP, BLOCK, 2 * HEAD), F32),
                pltpu.VMEM((BLOCK, BLOCK), F32),
                pltpu.VMEM((BLOCK, HEAD), BF16),
                pltpu.VMEM((3, BLOCK, HEAD), BF16),
                pltpu.SemaphoreType.DMA((KV,)),
                pltpu.SemaphoreType.DMA((KV,)),
                pltpu.SemaphoreType.DMA((KV,)),
                pltpu.SemaphoreType.DMA((KV,)),
                pltpu.SemaphoreType.DMA((3, KV)),
                pltpu.SemaphoreType.DMA((3, KV)),
            ],
            compiler_params=pltpu.CompilerParams(
                collective_id=0, has_side_effects=True, vmem_limit_bytes=62 * 2**20
            ),
        )(queries, keys, values, segment.reshape(1, BLOCK), signs.reshape(1, HEAD))

    placed = (
        P(("outer", "inner"), None),
        P(("outer", "inner"), None),
        P(("outer", "inner"), None),
        P(("outer", "inner")),
        P(),
    )
    return jax.shard_map(
        on_device, mesh=mesh, in_specs=placed, out_specs=P(("outer", "inner"), None), check_vma=False
    )
```

time: 100 us -> 40.6 us (0.41)
  the two profiles are of different devices: /device:TPU:75 before, /device:TPU:132 now
where the time goes in v1:
time: 40.6 us; the launch traced here: 40 us
  Pallas kernels  36.9 us (91%)
  local copies, waits for them, and re-layouts  3.13 us (8%)
    pallas_call x1, Pallas kernels, on_device(): pl.pallas_call(functools.partial(kernel, n_outer, n_inner), out_shape=jax...  36.9 us
    unnamed x1, local copies, waits for them, and re-layouts  3.13 us

profile of v1, /device:TPU:132, one launch (start us, length us, event | category | flops | bytes accessed | tf_op | source)
XLA Modules:
  0.0 40.0 jit_solution(12609701412127659162)
XLA Ops:
  0.0 36.9 %shard_map.55 = bf16[256,4096]{1,0:T(8,128)(2,1)} custom-call(bf16[256,4096]{1,0:T(8,128)(2,1)} %q_hbm.1, bf16[256,512]{1,0:T(8,128)(2,1)} %k_hbm.1, bf16[256,512]{1,0:T(8,128)(2,1)} %v_hbm.1, s32[1,256]{1,0:T(1,128)} %bitcast.2, s32[1,128]{1,0:T(1,128)} %bitcast.3), custom_call_target="tpu_custom_call" | custom-call | tf_op jit(solution)/shard_map/pallas_call | solution.py:183
  36.9 3.1 %copy.7 = bf16[256,4096]{1,0:T(8,128)(2,1)} copy(bf16[256,4096]{1,0:T(8,128)(2,1)} %shard_map.55) | data formatting | bytes 4194304

commit v2 on v1

--- a/solution.py
+++ b/solution.py
@@ -41,23 +41,56 @@
     return jnp.concatenate(parts, axis=0)
 
 
+def twice(block):
+    return jnp.concatenate([block, block], axis=1)
+
+
+def row_peak(first, second):
+    both = jnp.maximum(first, second)
+    both = jnp.maximum(both[:, :HEAD], both[:, HEAD:])
+    return jnp.broadcast_to(jnp.max(both, axis=1, keepdims=True), (BLOCK, HEAD))
+
+
 def kernel(
     n_outer, n_inner, q_hbm, k_hbm, v_hbm, seg_ref, signs_ref, o_hbm,
     q, raw, packs, out, top, acc, bias, away, docs,
     q_sem, k_sem, v_sem, o_sem, send, recv,
 ):
-    me = lax.axis_index("outer") * n_inner + lax.axis_index("inner")
     count = n_outer * n_inner
 
     def device(index):
         return {"outer": lax.div(index, n_inner), "inner": lax.rem(index, n_inner)}
 
-    offsets = (1, n_inner)
+    outer, inner = lax.axis_index("outer"), lax.axis_index("inner")
+    me = outer * n_inner + inner
+    even = lax.rem(outer, 2) == 0
+    odd = lax.rem(outer, 2) == 1
+    half = n_inner // 2
+    turn = inner == half - 1
+    wraps = odd & turn
+    late = (inner == half - 1) | (inner == n_inner - 1)
+    early = (inner == half - 2) | (inner == n_inner - 2)
+
+    has_near = me >= 1
+    has_hop = (me >= n_inner) | (me == half - 1)
+    has_far = me >= n_inner + 1
+    to_near = (me + 1 < count) & jnp.logical_not(wraps)
+    to_hop = (me + n_inner < count) | (me == count - half - 1)
+    to_back = even & turn
+    to_far = has_near & (me + n_inner < count)
+    to_far_late = to_far & jnp.logical_not(odd & late)
+    to_side = even & early & (me >= n_inner)
+
+    hop_index = lax.rem(me + n_inner, count)
+    back_index = lax.rem(me - n_inner + 1 + count, count)
+    hop_source = lax.rem(me - n_inner + count, count)
+    near_source = jnp.where(odd & (inner == half), lax.rem(me + n_inner - 1, count), me - 1)
+
     barrier = pltpu.get_barrier_semaphore()
-    for offset in offsets:
-        @pl.when(me >= offset)
+    for comes, source in ((has_near, near_source), (has_hop, hop_source)):
+        @pl.when(comes)
         def _():
-            pl.semaphore_signal(barrier, inc=1, device_id=device(me - offset), device_id_type=MESH)
+            pl.semaphore_signal(barrier, inc=1, device_id=device(source), device_id_type=MESH)
 
     def columns(h):
         return pl.ds(h * HEAD, HEAD)
@@ -82,31 +115,36 @@
         packs[0, h, 2 * BLOCK :, :] = own_rows
         k_in[h].wait()
 
-    for place, offset in ((1, 1), (2, n_inner), (3, n_inner + 1)):
-        @pl.when(me < offset)
+    for place, comes in ((1, has_near), (2, has_hop), (3, has_far)):
+        @pl.when(jnp.logical_not(comes))
         def _():
             for h in range(KV):
                 packs[place, h, : 2 * BLOCK, :] = jnp.zeros((2 * BLOCK, HEAD), BF16)
                 packs[place, h, 2 * BLOCK :, :] = jnp.full((16, HEAD), NO_DOC, BF16)
 
-    def carry(source, place, h, offset):
+    def carry(source, place, h, index, sent):
         return pltpu.make_async_remote_copy(
             src_ref=packs.at[source, h], dst_ref=packs.at[place, h],
-            send_sem=send.at[place - 1, h], recv_sem=recv.at[place - 1, h],
-            device_id=device(me + offset), device_id_type=MESH,
+            send_sem=send.at[sent, h], recv_sem=recv.at[place - 1, h],
+            device_id=device(index), device_id_type=MESH,
         )
 
-    near = [carry(0, 1, h, 1) for h in range(KV)]
-    hop = [carry(0, 2, h, n_inner) for h in range(KV)]
-    far = [carry(1, 3, h, n_inner) for h in range(KV)]
-    has_near, has_hop, has_far = me >= 1, me >= n_inner, me >= n_inner + 1
-    to_near, to_hop = me + 1 < count, me + n_inner < count
-    to_far = has_near & to_hop
-
-    pl.when(to_hop)(lambda: pl.semaphore_wait(barrier, 2))
-    pl.when(to_near & (me + n_inner >= count))(lambda: pl.semaphore_wait(barrier, 1))
+    near = [carry(0, 1, h, me + 1, 0) for h in range(KV)]
+    hop = [carry(0, 2, h, hop_index, 1) for h in range(KV)]
+    far = [carry(1, 3, h, me + n_inner, 2) for h in range(KV)]
+    back = [carry(2, 1, h, back_index, 3) for h in range(KV)]
+    side = [carry(2, 3, h, me + 1, 3) for h in range(KV)]
+
+    peers = to_near.astype(jnp.int32) + to_hop.astype(jnp.int32) + to_back.astype(jnp.int32)
+    for number in (1, 2, 3):
+        @pl.when(peers == number)
+        def _():
+            pl.semaphore_wait(barrier, number)
+    last = inner == n_inner - 1
+    first_near = odd | last
+    paced_near = jnp.logical_not(first_near | turn)
     for h in range(KV):
-        pl.when(to_near)(near[h].start)
+        pl.when(to_near & first_near)(near[h].start)
         pl.when(to_hop)(hop[h].start)
 
     own = documents(packs[0, 0, 2 * BLOCK :, :])
@@ -120,57 +158,85 @@
     def values_of(place, g):
         return jnp.concatenate([packs[place, g, BLOCK : 2 * BLOCK, :], ones], axis=1)
 
-    for g in range(KV):
+    def keys_of(place, g):
+        return jnp.concatenate([packs[place, g, :BLOCK, :], docs[place - 1]], axis=1)
+
+    def query_of(g, j):
+        return q[g, :, j * HEAD : (j + 1) * HEAD]
+
+    def read_documents(place, exists):
+        found = documents(packs[place, 0, 2 * BLOCK :, :])
+        none = (lax.broadcasted_iota(jnp.int32, (BLOCK, HEAD), 1) == NO_DOC).astype(F32)
+        docs[place - 1] = jnp.where(exists, found, none).astype(BF16)
+
+    def begin(g):
         q_in[g].wait()
+        pl.when(to_near & paced_near)(near[g].start)
+        pl.when(has_hop)(hop[g].wait_recv)
+        pl.when(to_back)(back[g].start)
+        pl.when(to_near & even & turn)(near[g].start)
+        if g >= KV // 2:
+            pl.when(to_side)(side[g].start)
+        if g == 0:
+            read_documents(2, me >= n_inner)
         for j in range(GROUP):
-            scores = lax.dot_general(
-                q[g, :, j * HEAD : (j + 1) * HEAD], packs[0, g, :BLOCK, :], ROW_BY_ROW, preferred_element_type=F32
-            ) + bias[...]
-            peak = jnp.max(scores, axis=1, keepdims=True)
-            weights = jnp.exp2((scores - peak) * SCALE).astype(BF16)
-            top[g * GROUP + j] = jnp.broadcast_to(peak, (BLOCK, HEAD))
-            acc[g * GROUP + j] = jnp.dot(weights, values_of(0, g), preferred_element_type=F32)
+            query = query_of(g, j)
+            wide_query = jnp.concatenate([query, away[...]], axis=1)
+            own_scores = lax.dot_general(query, packs[0, g, :BLOCK, :], ROW_BY_ROW, preferred_element_type=F32) + bias[...]
+            hop_scores = lax.dot_general(wide_query, keys_of(2, g), ROW_BY_ROW, preferred_element_type=F32)
+            peak = row_peak(own_scores, hop_scores)
+            total = None
+            for place, scores in ((0, own_scores), (2, hop_scores)):
+                weights = jnp.exp2((scores - twice(peak)) * SCALE).astype(BF16)
+                part = jnp.dot(weights, values_of(place, g), preferred_element_type=F32)
+                total = part if total is None else total + part
+            top[g * GROUP + j] = peak
+            acc[g * GROUP + j] = total
 
     def arrive(h):
         pl.when(has_near)(near[h].wait_recv)
-        pl.when(to_far)(far[h].start)
-
-    def attend(g):
-        pl.when(has_hop)(hop[g].wait_recv)
+        pl.when(to_far if h < KV // 2 else to_far_late)(far[h].start)
+
+    def finish(g):
         pl.when(has_far)(far[g].wait_recv)
         if g == 0:
-            for place in (1, 2, 3):
-                docs[place - 1] = documents(packs[place, 0, 2 * BLOCK :, :]).astype(BF16)
+            read_documents(1, me >= 1)
+            read_documents(3, me >= n_inner + 1)
         for j in range(GROUP):
-            query = jnp.concatenate([q[g, :, j * HEAD : (j + 1) * HEAD], away[...]], axis=1)
-            scores = []
-            for place in (1, 2, 3):
-                key = jnp.concatenate([packs[place, g, :BLOCK, :], docs[place - 1]], axis=1)
-                scores.append(lax.dot_general(query, key, ROW_BY_ROW, preferred_element_type=F32))
-            before = top[g * GROUP + j][:, :1]
-            peak = jnp.max(functools.reduce(jnp.maximum, scores), axis=1, keepdims=True)
-            peak = jnp.maximum(peak, before)
-            total = acc[g * GROUP + j] * jnp.exp2((before - peak) * SCALE)
-            for place in (1, 2, 3):
-                weights = jnp.exp2((scores[place - 1] - peak) * SCALE).astype(BF16)
+            query = jnp.concatenate([query_of(g, j), away[...]], axis=1)
+            scores = [
+                lax.dot_general(query, keys_of(place, g), ROW_BY_ROW, preferred_element_type=F32) for place in (1, 3)
+            ]
+            before = top[g * GROUP + j]
+            peak = jnp.maximum(row_peak(*scores), before)
+            total = acc[g * GROUP + j] * twice(jnp.exp2((before - peak) * SCALE))
+            for place, score in zip((1, 3), scores):
+                weights = jnp.exp2((score - twice(peak)) * SCALE).astype(BF16)
                 total = total + jnp.dot(weights, values_of(place, g), preferred_element_type=F32)
-            out[g, :, j * HEAD : (j + 1) * HEAD] = (total[:, :HEAD] / total[:, HEAD:]).astype(BF16)
+            mass = total[:, HEAD:]
+            share = pl.reciprocal(mass, approx=True)
+            share = share * (2 - mass * share)
+            out[g, :, j * HEAD : (j + 1) * HEAD] = (total[:, :HEAD] * share).astype(BF16)
         copy = pltpu.make_async_copy(out.at[g], o_hbm.at[:, pl.ds(g * wide, wide)], o_sem.at[g])
         copy.start()
         return copy
 
+    for g in range(KV):
+        begin(g)
     arrive(0)
     arrive(1)
-    outs = [attend(0)]
+    outs = [finish(0)]
     arrive(2)
-    outs.append(attend(1))
+    outs.append(finish(1))
     arrive(3)
-    outs.append(attend(2))
-    outs.append(attend(3))
+    outs += [finish(2), finish(3)]
     for h in range(KV):
         pl.when(to_near)(near[h].wait_send)
         pl.when(to_hop)(hop[h].wait_send)
-        pl.when(to_far)(far[h].wait_send)
+        pl.when(to_far if h < KV // 2 else to_far_late)(far[h].wait_send)
+        pl.when(to_back)(back[h].wait_send)
+        if h >= KV // 2:
+            pl.when(to_side)(side[h].wait_send)
         outs[h].wait()
 
 
@@ -182,7 +248,7 @@
         here = pl.BlockSpec(memory_space=pltpu.VMEM)
         return pl.pallas_call(
             functools.partial(kernel, n_outer, n_inner),
-            out_shape=jax.ShapeDtypeStruct(queries.shape, BF16),
+            out_shape=pltpu.VMEM(queries.shape, BF16),
             in_specs=[anywhere, anywhere, anywhere, here, here],
             out_specs=anywhere,
             scratch_shapes=[
@@ -199,11 +265,11 @@
                 pltpu.SemaphoreType.DMA((KV,)),
                 pltpu.SemaphoreType.DMA((KV,)),
                 pltpu.SemaphoreType.DMA((KV,)),
-                pltpu.SemaphoreType.DMA((3, KV)),
+                pltpu.SemaphoreType.DMA((4, KV)),
                 pltpu.SemaphoreType.DMA((3, KV)),
             ],
             compiler_params=pltpu.CompilerParams(
-                collective_id=0, has_side_effects=True, vmem_limit_bytes=62 * 2**20
+                collective_id=0, has_side_effects=True, vmem_limit_bytes=60 * 2**20
             ),
         )(queries, keys, values, segment.reshape(1, BLOCK), signs.reshape(1, HEAD))
 

time: 40.6 us -> 31.3 us (0.77)
  the two profiles are of different devices: /device:TPU:132 before, /device:TPU:164 now
where the time goes in v2:
time: 31.3 us; the launch traced here: 31.1 us
  Pallas kernels  29.8 us (95%)
  local copies, waits for them, and re-layouts  1.32 us (4%)
    pallas_call x1, Pallas kernels, on_device(): pl.pallas_call(functools.partial(kernel, n_outer, n_inner), out_shape=plt...  29.8 us
    unnamed x1, local copies, waits for them, and re-layouts  1.32 us

profile of v2, /device:TPU:164, one launch (start us, length us, event | category | flops | bytes accessed | tf_op | source)
XLA Modules:
  0.0 31.1 jit_solution(10649317246796027775)
XLA Ops:
  0.0 29.8 %shard_map.55 = bf16[256,4096]{1,0:T(8,128)(2,1)S(1)} custom-call(bf16[256,4096]{1,0:T(8,128)(2,1)} %q_hbm.1, bf16[256,512]{1,0:T(8,128)(2,1)} %k_hbm.1, bf16[256,512]{1,0:T(8,128)(2,1)} %v_hbm.1, s32[1,256]{1,0:T(1,128)} %bitcast.2, s32[1,128]{1,0:T(1,128)} %bitcast.3), custom_call_target="tpu_custom_call" | custom-call | tf_op jit(solution)/shard_map/pallas_call | solution.py:249
  29.8 1.3 %copy.7 = bf16[256,4096]{1,0:T(8,128)(2,1)} copy(bf16[256,4096]{1,0:T(8,128)(2,1)S(1)} %shard_map.55) | data formatting | bytes 4194304

commit v3 on v2

--- a/solution.py
+++ b/solution.py
@@ -52,9 +52,9 @@
 
 
 def kernel(
-    n_outer, n_inner, q_hbm, k_hbm, v_hbm, seg_ref, signs_ref, o_hbm,
-    q, raw, packs, out, top, acc, bias, away, docs,
-    q_sem, k_sem, v_sem, o_sem, send, recv,
+    n_outer, n_inner, q_hbm, k_hbm, v_hbm, seg_ref, signs_ref, out,
+    q, raw, packs, top, acc, bias, away, docs,
+    q_sem, k_sem, v_sem, send, recv,
 ):
     count = n_outer * n_inner
 
@@ -80,6 +80,8 @@
     to_far = has_near & (me + n_inner < count)
     to_far_late = to_far & jnp.logical_not(odd & late)
     to_side = even & early & (me >= n_inner)
+    to_side_first = to_side & (inner == half - 2)
+    to_far_first = to_far & jnp.logical_not(odd & turn)
 
     hop_index = lax.rem(me + n_inner, count)
     back_index = lax.rem(me - n_inner + 1 + count, count)
@@ -175,8 +177,7 @@
         pl.when(has_hop)(hop[g].wait_recv)
         pl.when(to_back)(back[g].start)
         pl.when(to_near & even & turn)(near[g].start)
-        if g >= KV // 2:
-            pl.when(to_side)(side[g].start)
+        pl.when(to_side_first if g < KV // 2 else to_side)(side[g].start)
         if g == 0:
             read_documents(2, me >= n_inner)
         for j in range(GROUP):
@@ -193,51 +194,59 @@
             top[g * GROUP + j] = peak
             acc[g * GROUP + j] = total
 
-    def arrive(h):
-        pl.when(has_near)(near[h].wait_recv)
-        pl.when(to_far if h < KV // 2 else to_far_late)(far[h].start)
+    def arrive(h, here):
+        pl.when(has_near & here)(near[h].wait_recv)
+        pl.when((to_far_first if h < KV // 2 else to_far_late) & here)(far[h].start)
+
+    def merged(place, g, j):
+        query = jnp.concatenate([query_of(g, j), away[...]], axis=1)
+        scores = lax.dot_general(query, keys_of(place, g), ROW_BY_ROW, preferred_element_type=F32)
+        before = top[g * GROUP + j]
+        peak = jnp.maximum(row_peak(scores, scores), before)
+        weights = jnp.exp2((scores - twice(peak)) * SCALE).astype(BF16)
+        part = jnp.dot(weights, values_of(place, g), preferred_element_type=F32)
+        return acc[g * GROUP + j] * twice(jnp.exp2((before - peak) * SCALE)) + part, peak
+
+    def extend(g):
+        if g == 0:
+            read_documents(1, me >= 1)
+        for j in range(GROUP):
+            acc[g * GROUP + j], top[g * GROUP + j] = merged(1, g, j)
 
     def finish(g):
         pl.when(has_far)(far[g].wait_recv)
         if g == 0:
-            read_documents(1, me >= 1)
             read_documents(3, me >= n_inner + 1)
         for j in range(GROUP):
-            query = jnp.concatenate([query_of(g, j), away[...]], axis=1)
-            scores = [
-                lax.dot_general(query, keys_of(place, g), ROW_BY_ROW, preferred_element_type=F32) for place in (1, 3)
-            ]
-            before = top[g * GROUP + j]
-            peak = jnp.maximum(row_peak(*scores), before)
-            total = acc[g * GROUP + j] * twice(jnp.exp2((before - peak) * SCALE))
-            for place, score in zip((1, 3), scores):
-                weights = jnp.exp2((score - twice(peak)) * SCALE).astype(BF16)
-                total = total + jnp.dot(weights, values_of(place, g), preferred_element_type=F32)
+            total, _ = merged(3, g, j)
             mass = total[:, HEAD:]
             share = pl.reciprocal(mass, approx=True)
             share = share * (2 - mass * share)
-            out[g, :, j * HEAD : (j + 1) * HEAD] = (total[:, :HEAD] * share).astype(BF16)
-        copy = pltpu.make_async_copy(out.at[g], o_hbm.at[:, pl.ds(g * wide, wide)], o_sem.at[g])
-        copy.start()
-        return copy
-
+            out[:, (g * GROUP + j) * HEAD : (g * GROUP + j + 1) * HEAD] = (total[:, :HEAD] * share).astype(BF16)
+
+    early_near = even & last
+    later = jnp.logical_not(early_near)
     for g in range(KV):
         begin(g)
-    arrive(0)
-    arrive(1)
-    outs = [finish(0)]
-    arrive(2)
-    outs.append(finish(1))
-    arrive(3)
-    outs += [finish(2), finish(3)]
+        arrive(g, early_near)
+    arrive(0, later)
+    extend(0)
+    arrive(1, later)
+    finish(0)
+    extend(1)
+    arrive(2, later)
+    finish(1)
+    extend(2)
+    arrive(3, later)
+    finish(2)
+    extend(3)
+    finish(3)
     for h in range(KV):
         pl.when(to_near)(near[h].wait_send)
         pl.when(to_hop)(hop[h].wait_send)
-        pl.when(to_far if h < KV // 2 else to_far_late)(far[h].wait_send)
+        pl.when(to_far_first if h < KV // 2 else to_far_late)(far[h].wait_send)
         pl.when(to_back)(back[h].wait_send)
-        if h >= KV // 2:
-            pl.when(to_side)(side[h].wait_send)
-        outs[h].wait()
+        pl.when(to_side_first if h < KV // 2 else to_side)(side[h].wait_send)
 
 
 def solution(mesh):
@@ -250,18 +259,16 @@
             functools.partial(kernel, n_outer, n_inner),
             out_shape=pltpu.VMEM(queries.shape, BF16),
             in_specs=[anywhere, anywhere, anywhere, here, here],
-            out_specs=anywhere,
+            out_specs=here,
             scratch_shapes=[
                 pltpu.VMEM((KV, BLOCK, GROUP * HEAD), BF16),
                 pltpu.VMEM((KV, BLOCK, HEAD), BF16),
                 pltpu.VMEM((4, KV, ROWS, HEAD), BF16),
-                pltpu.VMEM((KV, BLOCK, GROUP * HEAD), BF16),
                 pltpu.VMEM((KV * GROUP, BLOCK, HEAD), F32),
                 pltpu.VMEM((KV * GROUP, BLOCK, 2 * HEAD), F32),
                 pltpu.VMEM((BLOCK, BLOCK), F32),
                 pltpu.VMEM((BLOCK, HEAD), BF16),
                 pltpu.VMEM((3, BLOCK, HEAD), BF16),
-                pltpu.SemaphoreType.DMA((KV,)),
                 pltpu.SemaphoreType.DMA((KV,)),
                 pltpu.SemaphoreType.DMA((KV,)),
                 pltpu.SemaphoreType.DMA((KV,)),

time: 31.3 us -> 29.9 us (0.955)
  the two profiles are of different devices: /device:TPU:164 before, /device:TPU:132 now
where the time goes in v3:
time: 29.9 us; the launch traced here: 29.8 us
  Pallas kernels  28.5 us (95%)
  local copies, waits for them, and re-layouts  1.32 us (4%)
    pallas_call x1, Pallas kernels, on_device(): pl.pallas_call(functools.partial(kernel, n_outer, n_inner), out_shape=plt...  28.5 us
    unnamed x1, local copies, waits for them, and re-layouts  1.32 us

profile of v3, /device:TPU:132, one launch (start us, length us, event | category | flops | bytes accessed | tf_op | source)
XLA Modules:
  0.0 29.8 jit_solution(3390556313027728439)
XLA Ops:
  0.0 28.5 %shard_map.55 = bf16[256,4096]{1,0:T(8,128)(2,1)S(1)} custom-call(bf16[256,4096]{1,0:T(8,128)(2,1)} %q_hbm.1, bf16[256,512]{1,0:T(8,128)(2,1)} %k_hbm.1, bf16[256,512]{1,0:T(8,128)(2,1)} %v_hbm.1, s32[1,256]{1,0:T(1,128)} %bitcast.2, s32[1,128]{1,0:T(1,128)} %bitcast.3), custom_call_target="tpu_custom_call" | custom-call | tf_op jit(solution)/shard_map/pallas_call | solution.py:258
  28.5 1.3 %copy.7 = bf16[256,4096]{1,0:T(8,128)(2,1)} copy(bf16[256,4096]{1,0:T(8,128)(2,1)S(1)} %shard_map.55) | data formatting | bytes 4194304

commit v4 on v3

--- a/solution.py
+++ b/solution.py
@@ -110,42 +110,44 @@
     flips = (1 - 2 * signs_ref[...]).astype(F32)
     table = hadamard_signs()
 
+    for place, comes in ((1, has_near), (2, has_hop), (3, has_far)):
+        @pl.when(jnp.logical_not(comes))
+        def _():
+            for h in range(KV):
+                packs[place, h, : 2 * BLOCK, :] = jnp.zeros((2 * BLOCK, HEAD), BF16)
+                packs[place, h, 2 * BLOCK :, :] = jnp.full((16, HEAD), NO_DOC, BF16)
+
+    def carry(source, place, h, index, sent):
+        return pltpu.make_async_remote_copy(
+            src_ref=packs.at[source, h], dst_ref=packs.at[place, h],
+            send_sem=send.at[sent, h], recv_sem=recv.at[place - 1, h],
+            device_id=device(index), device_id_type=MESH,
+        )
+
+    near = [carry(0, 1, h, me + 1, 0) for h in range(KV)]
+    hop = [carry(0, 2, h, hop_index, 1) for h in range(KV)]
+    far = [carry(1, 3, h, me + n_inner, 2) for h in range(KV)]
+    back = [carry(2, 1, h, back_index, 3) for h in range(KV)]
+    side = [carry(2, 3, h, me + 1, 3) for h in range(KV)]
+
+    peers = to_near.astype(jnp.int32) + to_hop.astype(jnp.int32) + to_back.astype(jnp.int32)
+    def all_here():
+        for number in (1, 2, 3):
+            @pl.when(peers == number)
+            def _():
+                pl.semaphore_wait(barrier, number)
+
+    last = inner == n_inner - 1
+    first_near = odd | last
+    paced_near = jnp.logical_not(first_near | turn)
     for h in range(KV):
         v_in[h].wait()
         turned = jnp.dot((raw[h].astype(F32) * flips).astype(BF16), table, preferred_element_type=F32)
         packs[0, h, BLOCK : 2 * BLOCK, :] = (turned * F32(1 / math.sqrt(HEAD))).astype(BF16)
         packs[0, h, 2 * BLOCK :, :] = own_rows
         k_in[h].wait()
-
-    for place, comes in ((1, has_near), (2, has_hop), (3, has_far)):
-        @pl.when(jnp.logical_not(comes))
-        def _():
-            for h in range(KV):
-                packs[place, h, : 2 * BLOCK, :] = jnp.zeros((2 * BLOCK, HEAD), BF16)
-                packs[place, h, 2 * BLOCK :, :] = jnp.full((16, HEAD), NO_DOC, BF16)
-
-    def carry(source, place, h, index, sent):
-        return pltpu.make_async_remote_copy(
-            src_ref=packs.at[source, h], dst_ref=packs.at[place, h],
-            send_sem=send.at[sent, h], recv_sem=recv.at[place - 1, h],
-            device_id=device(index), device_id_type=MESH,
-        )
-
-    near = [carry(0, 1, h, me + 1, 0) for h in range(KV)]
-    hop = [carry(0, 2, h, hop_index, 1) for h in range(KV)]
-    far = [carry(1, 3, h, me + n_inner, 2) for h in range(KV)]
-    back = [carry(2, 1, h, back_index, 3) for h in range(KV)]
-    side = [carry(2, 3, h, me + 1, 3) for h in range(KV)]
-
-    peers = to_near.astype(jnp.int32) + to_hop.astype(jnp.int32) + to_back.astype(jnp.int32)
-    for number in (1, 2, 3):
-        @pl.when(peers == number)
-        def _():
-            pl.semaphore_wait(barrier, number)
-    last = inner == n_inner - 1
-    first_near = odd | last
-    paced_near = jnp.logical_not(first_near | turn)
-    for h in range(KV):
+        if h == 0:
+            all_here()
         pl.when(to_near & first_near)(near[h].start)
         pl.when(to_hop)(hop[h].start)
 

time: 29.9 us -> 29.9 us (level)
  no operation moved by 1% of the time
where the time goes in v4:
time: 29.9 us; the launch traced here: 29.8 us
  Pallas kernels  28.5 us (95%)
  local copies, waits for them, and re-layouts  1.32 us (4%)
    pallas_call x1, Pallas kernels, on_device(): pl.pallas_call(functools.partial(kernel, n_outer, n_inner), out_shape=plt...  28.5 us
    unnamed x1, local copies, waits for them, and re-layouts  1.32 us

profile of v4, /device:TPU:132, one launch (start us, length us, event | category | flops | bytes accessed | tf_op | source)
XLA Modules:
  0.0 29.8 jit_solution(12949791615923161092)
XLA Ops:
  0.0 28.5 %shard_map.55 = bf16[256,4096]{1,0:T(8,128)(2,1)S(1)} custom-call(bf16[256,4096]{1,0:T(8,128)(2,1)} %q_hbm.1, bf16[256,512]{1,0:T(8,128)(2,1)} %k_hbm.1, bf16[256,512]{1,0:T(8,128)(2,1)} %v_hbm.1, s32[1,256]{1,0:T(1,128)} %bitcast.2, s32[1,128]{1,0:T(1,128)} %bitcast.3), custom_call_target="tpu_custom_call" | custom-call | tf_op jit(solution)/shard_map/pallas_call | solution.py:260
  28.5 1.3 %copy.7 = bf16[256,4096]{1,0:T(8,128)(2,1)} copy(bf16[256,4096]{1,0:T(8,128)(2,1)S(1)} %shard_map.55) | data formatting | bytes 4194304

commit v5 on v4

--- a/solution.py
+++ b/solution.py
@@ -65,6 +65,7 @@
     me = outer * n_inner + inner
     even = lax.rem(outer, 2) == 0
     odd = lax.rem(outer, 2) == 1
+    low = lax.rem(lax.div(outer, 2), 2)
     half = n_inner // 2
     turn = inner == half - 1
     wraps = odd & turn
@@ -81,6 +82,8 @@
     to_far_late = to_far & jnp.logical_not(odd & late)
     to_side = even & early & (me >= n_inner)
     to_side_first = to_side & (inner == half - 2)
+    to_side_last = to_side | (even & turn & (low == 0) & (me >= n_inner))
+    to_far_last = to_far_late & jnp.logical_not(odd & (inner == half) & (low == 1))
     to_far_first = to_far & jnp.logical_not(odd & turn)
 
     hop_index = lax.rem(me + n_inner, count)
@@ -128,7 +131,7 @@
     hop = [carry(0, 2, h, hop_index, 1) for h in range(KV)]
     far = [carry(1, 3, h, me + n_inner, 2) for h in range(KV)]
     back = [carry(2, 1, h, back_index, 3) for h in range(KV)]
-    side = [carry(2, 3, h, me + 1, 3) for h in range(KV)]
+    side = [carry(2, 3, h, me + 1, 4) for h in range(KV)]
 
     peers = to_near.astype(jnp.int32) + to_hop.astype(jnp.int32) + to_back.astype(jnp.int32)
     def all_here():
@@ -179,7 +182,7 @@
         pl.when(has_hop)(hop[g].wait_recv)
         pl.when(to_back)(back[g].start)
         pl.when(to_near & even & turn)(near[g].start)
-        pl.when(to_side_first if g < KV // 2 else to_side)(side[g].start)
+        pl.when((to_side_first, to_side_first, to_side, to_side_last)[g])(side[g].start)
         if g == 0:
             read_documents(2, me >= n_inner)
         for j in range(GROUP):
@@ -198,7 +201,7 @@
 
     def arrive(h, here):
         pl.when(has_near & here)(near[h].wait_recv)
-        pl.when((to_far_first if h < KV // 2 else to_far_late) & here)(far[h].start)
+        pl.when((to_far_first, to_far_first, to_far_late, to_far_last)[h] & here)(far[h].start)
 
     def merged(place, g, j):
         query = jnp.concatenate([query_of(g, j), away[...]], axis=1)
@@ -246,9 +249,9 @@
     for h in range(KV):
         pl.when(to_near)(near[h].wait_send)
         pl.when(to_hop)(hop[h].wait_send)
-        pl.when(to_far_first if h < KV // 2 else to_far_late)(far[h].wait_send)
+        pl.when((to_far_first, to_far_first, to_far_late, to_far_last)[h])(far[h].wait_send)
         pl.when(to_back)(back[h].wait_send)
-        pl.when(to_side_first if h < KV // 2 else to_side)(side[h].wait_send)
+        pl.when((to_side_first, to_side_first, to_side, to_side_last)[h])(side[h].wait_send)
 
 
 def solution(mesh):
@@ -274,7 +277,7 @@
                 pltpu.SemaphoreType.DMA((KV,)),
                 pltpu.SemaphoreType.DMA((KV,)),
                 pltpu.SemaphoreType.DMA((KV,)),
-                pltpu.SemaphoreType.DMA((4, KV)),
+                pltpu.SemaphoreType.DMA((5, KV)),
                 pltpu.SemaphoreType.DMA((3, KV)),
             ],
             compiler_params=pltpu.CompilerParams(

time: 29.9 us -> 29.7 us (level); the launches traced: 29.8 us -> 29.2 us
  Pallas kernels: 28.5 us -> 27.9 us
    pallas_call x1, Pallas kernels: 28.5 us -> 27.9 us  [on_device(): pl.pallas_call(functools.partial(kernel, n_outer, n_inner), out_shape=plt...]
where the time goes in v5:
time: 29.7 us; the launch traced here: 29.2 us
  Pallas kernels  27.9 us (94%)
  local copies, waits for them, and re-layouts  1.32 us (4%)
    pallas_call x1, Pallas kernels, on_device(): pl.pallas_call(functools.partial(kernel, n_outer, n_inner), out_shape=plt...  27.9 us
    unnamed x1, local copies, waits for them, and re-layouts  1.32 us

profile of v5, /device:TPU:132, one launch (start us, length us, event | category | flops | bytes accessed | tf_op | source)
XLA Modules:
  0.0 29.2 jit_solution(13281193250012076131)
XLA Ops:
  0.0 27.9 %shard_map.55 = bf16[256,4096]{1,0:T(8,128)(2,1)S(1)} custom-call(bf16[256,4096]{1,0:T(8,128)(2,1)} %q_hbm.1, bf16[256,512]{1,0:T(8,128)(2,1)} %k_hbm.1, bf16[256,512]{1,0:T(8,128)(2,1)} %v_hbm.1, s32[1,256]{1,0:T(1,128)} %bitcast.2, s32[1,128]{1,0:T(1,128)} %bitcast.3), custom_call_target="tpu_custom_call" | custom-call | tf_op jit(solution)/shard_map/pallas_call | solution.py:263
  27.9 1.3 %copy.7 = bf16[256,4096]{1,0:T(8,128)(2,1)} copy(bf16[256,4096]{1,0:T(8,128)(2,1)S(1)} %shard_map.55) | data formatting | bytes 4194304
